TPU v7x, 256 devices: a whole 4x4x8 slice. The times are simulated.
256 devices in a mesh: seq: 128 (over x, y_hi, z, core), section: 2 (over y_lo).
Axes of the slice: x: 4, y: 4 (y_hi: 2, y_lo: 2; y = y_hi * 2 + y_lo), z: 8, core: 2. Of those that a mesh axis runs over, the one named last changes fastest.
Arguments:
- hidden: bfloat16 [2, 2, 2048, 3072], P('section', None, 'seq'), may hold values from -2 to 2
- image_qkv: bfloat16 [2, 2, 2048, 3, 2048], P('section', None, 'seq'), may hold values from -6 to 6
- text_slots: bfloat16 [2, 2, 128, 3, 256, 2048], P('section', None, 'seq'), may hold values from -6 to 6
- norm_gains: float32 [2, 4, 128], P('section'), may hold values from 0.7 to 2.2
- out_weight: bfloat16 [2, 2048, 3072], P('section', 'seq'), may hold values from -0.125 to 0.125
- gate: float32 [2, 4, 3072], P('section'), may hold values from 1 to 4
- owner: int32 [4], replicated, may hold values from 0 to 127
- plan: int32 [4], replicated, may hold values from 0 to 3, each once
Outputs:
- handed: bfloat16 [2, 2, 2048, 3072], P('section', None, 'seq')
- text_attn: bfloat16 [2, 128, 2, 32, 128], P('section', 'seq')
Inputs may be any that keep to these rules, and one draw needn't show every extreme that they name: `plan`: each prompt appears once.
All inputs are finite; a program needn't handle non-finite values.
Results may differ from a plain program's by a relative error of at most 0.0095.
Values may be sent and summed in bfloat16 or wider, within the bound.
A program may use at most 128 MiB of HBM per device.

v0:
```python
import math

import jax
import jax.numpy as jnp
import numpy as np
from jax import lax
from jax.sharding import PartitionSpec as P

COLS = 128


EPSILON = 1e-06
THETA = 10000.0


def from_root(block, axis, owner):
    block = jnp.where(lax.axis_index(axis) == owner, block, jnp.zeros_like(block))
    return lax.psum(block, axis)


def shifted(block, axis, distance):
    devices = range(lax.axis_size(axis))
    route = [((i - distance) % len(devices), i) for i in devices]
    return lax.ppermute(block, axis, route)


def rope_angles(head_size, row_pos, col_pos):
    time_dims = head_size // 8
    space_dims = (head_size - time_dims) // 2
    frequency = np.exp(-math.log(THETA) * np.arange(0, space_dims, 2) / space_dims).astype(
        np.float32
    )
    still_part = jnp.zeros((row_pos.shape[0], time_dims // 2), row_pos.dtype)
    angles = jnp.concatenate(
        [still_part, row_pos[:, None] * frequency[None, :], col_pos[:, None] * frequency[None, :]],
        axis=1,
    )
    return (jnp.cos(angles), jnp.sin(angles))


def normalize(raw_values, gain_vec):
    field = raw_values.astype(jnp.float32)
    return field * lax.rsqrt(jnp.mean(field * field, axis=-1, keepdims=True) + EPSILON) * gain_vec


def rotate(field, cosine, sine_table):
    half_size = field.shape[-1] // 2
    paired = field.reshape(field.shape[:-1] + (half_size, 2))
    even_part = paired[..., 0]
    odd_part = paired[..., 1]
    cos_b = cosine[:, None, :]
    sin_b = sine_table[:, None, :]
    turned = jnp.stack(
        [even_part * cos_b - odd_part * sin_b, even_part * sin_b + odd_part * cos_b], axis=-1
    )
    return turned.reshape(field.shape)


def attend(queries, text_k, text_v, image_k, image_v, block_width):
    score_scale = 1.0 / math.sqrt(queries.shape[-1])
    first_scores = (
        jnp.einsum("qd,kd->qk", queries, text_k, preferred_element_type=jnp.float32) * score_scale
    )
    first_weights = jnp.exp(first_scores)
    denominator = jnp.sum(first_weights, axis=1)
    numerator = jnp.dot(
        first_weights.astype(jnp.bfloat16), text_v, preferred_element_type=jnp.float32
    )
    block_count = image_k.shape[0] // block_width

    def one_block(block_index, carried):
        running_num, running_den = carried
        scores = (
            jnp.einsum("qd,kd->qk", queries, image_k, preferred_element_type=jnp.float32)
            * score_scale
        )
        weights = jnp.exp(scores)
        running_num = running_num + jnp.dot(
            weights.astype(jnp.bfloat16), image_v, preferred_element_type=jnp.float32
        )
        return (running_num, running_den + jnp.sum(weights, axis=1))

    numerator, denominator = lax.fori_loop(0, block_count, one_block, (numerator, denominator))
    return (numerator / denominator[:, None]).astype(jnp.bfloat16)


def per_device(hidden, image_qkv, text_slots, norm_gains, out_weight, gate, owner, plan):
    seq_count = lax.axis_size("seq")
    section_index = lax.axis_index("section")
    seq_index = lax.axis_index("seq")
    micros = hidden.shape[1]
    local_tokens = hidden.shape[2]
    model_width = hidden.shape[3]
    inner_width = image_qkv.shape[-1]
    head_size = norm_gains.shape[-1]
    head_count = inner_width // head_size
    group_count = seq_count // head_count
    group_rows = local_tokens // group_count
    head_index = seq_index // group_count
    group_index = seq_index % group_count
    text_len = text_slots.shape[4]
    text_rows = text_len // group_count
    total_tokens = local_tokens * seq_count
    norm_gain = norm_gains[0]
    positions = seq_index * local_tokens + jnp.arange(local_tokens, dtype=jnp.int32)
    row_pos = (positions // COLS).astype(jnp.float32)
    col_pos = (positions % COLS).astype(jnp.float32)
    cosine, sine_table = rope_angles(head_size, row_pos, col_pos)
    image_data = image_qkv[0]
    shaped = (micros, local_tokens, head_count, head_size)
    query_local = rotate(
        normalize(image_data[:, :, 0].reshape(shaped), norm_gain[0]), cosine, sine_table
    ).astype(jnp.bfloat16)
    key_local = rotate(
        normalize(image_data[:, :, 1].reshape(shaped), norm_gain[1]), cosine, sine_table
    ).astype(jnp.bfloat16)
    value_local = image_data[:, :, 2].reshape(shaped)
    query_send = query_local.reshape(micros, group_count, group_rows, head_count, head_size)
    query_send = query_send.transpose(3, 1, 0, 2, 4).reshape(
        seq_count, micros, group_rows, head_size
    )
    pair_local = jnp.stack([key_local, value_local], axis=0)
    pair_heads = pair_local.transpose(3, 0, 1, 2, 4)[:, None]
    pair_send = jnp.broadcast_to(
        pair_heads, (head_count, group_count, 2, micros, local_tokens, head_size)
    )
    pair_send = pair_send.reshape(seq_count, 2, micros, local_tokens, head_size)
    query_recv, pair_recv = (
        lax.all_to_all(query_send, "seq", split_axis=0, concat_axis=0, tiled=True),
        lax.all_to_all(pair_send, "seq", split_axis=0, concat_axis=0, tiled=True),
    )
    key_value = pair_recv.transpose(1, 2, 0, 3, 4).reshape(2, micros, total_tokens, head_size)
    block_width = math.gcd(total_tokens, 2048)
    image_parts = []
    text_parts = []
    for micro_index in range(micros):
        prompt_index = plan[section_index * micros + micro_index]
        owner_index = owner[prompt_index]
        text_slot = from_root(text_slots[0, micro_index, 0], "seq", owner_index)
        head_slot = lax.dynamic_slice_in_dim(text_slot, head_index * head_size, head_size, 2)
        text_query_rows = lax.dynamic_slice_in_dim(
            head_slot[0], group_index * text_rows, text_rows, 0
        )
        text_q = normalize(text_query_rows, norm_gain[2]).astype(jnp.bfloat16)
        text_k = normalize(head_slot[1], norm_gain[3]).astype(jnp.bfloat16)
        text_v = head_slot[2]
        image_queries = query_recv[:, micro_index].reshape(seq_count * group_rows, head_size)
        queries = jnp.concatenate([text_q, image_queries], axis=0)
        attended_rows = attend(
            queries,
            text_k,
            text_v,
            key_value[0, micro_index],
            key_value[1, micro_index],
            block_width,
        )
        text_parts.append(attended_rows[:text_rows])
        image_parts.append(attended_rows[text_rows:].reshape(seq_count, group_rows, head_size))
    returned = lax.all_to_all(
        jnp.stack(image_parts, axis=1), "seq", split_axis=0, concat_axis=0, tiled=True
    )
    attended = returned.reshape(head_count, group_count, micros, group_rows, head_size)
    attended = attended.transpose(2, 1, 3, 0, 4).reshape(micros * local_tokens, inner_width)
    projected = jnp.dot(
        attended,
        lax.all_gather(out_weight[0], "seq", axis=0, tiled=True),
        preferred_element_type=jnp.float32,
    )
    chosen = lax.dynamic_slice_in_dim(plan, section_index * micros, micros)
    gate_rows = jnp.take(gate[0], chosen, axis=0)
    block_out = (
        hidden[0].astype(jnp.float32)
        + gate_rows[:, None, :] * projected.reshape(micros, local_tokens, model_width)
    ).astype(jnp.bfloat16)
    handed = shifted(block_out, "section", 1)
    return (handed[None], jnp.stack(text_parts, axis=0)[None, None])


def solution(mesh):
    return jax.shard_map(
        per_device,
        mesh=mesh,
        in_specs=(
            P("section", None, "seq", None),
            P("section", None, "seq", None, None),
            P("section", None, "seq", None, None, None),
            P("section", None, None),
            P("section", "seq", None),
            P("section", None, None),
            P(),
            P(),
        ),
        out_specs=(P("section", None, "seq", None), P("section", "seq", None, None, None)),
        check_vma=False,
    )
```

profile of v0, /device:TPU:1, one launch (start us, length us, event | category | flops | bytes accessed | tf_op | source)
XLA Modules:
  0.0 1474.9 jit_solution(12203735505310509130)
XLA Ops:
  7.2 0.0 copy-start
  7.2 0.0 all-reduce.3.cloned.1.call-start
  7.2 1.3 fusion.75
  12.4 1.3 fusion.74
  15.1 4.7 select_bitcast_fusion.1
  19.8 0.0 all-reduce.3.cloned.1.call-update
  19.8 0.0 all-gather.3.cloned.1.call-start
  19.9 0.7 all-gather.3.cloned.1.call-update
  20.6 0.2 copy-done.2
  20.8 0.6 copy.58
  21.5 0.1 mul.313
  21.7 0.0 copy-start.6
  21.7 0.1 bitcast_reduce_fusion
  21.9 0.1 copy.59
  22.0 0.1 mul.284
  22.1 2.0 copy.51
  24.1 0.1 bitcast_reduce_fusion.1
  24.3 0.1 copy.52
  24.4 0.1 broadcast_multiply_fusion.1
  24.5 0.1 fusion.62
  24.6 0.1 copy.54
  24.7 0.1 copy.53
  24.8 3.9 multiply_multiply_fusion
  28.7 6.2 subtract_convert_fusion
  34.9 2.8 pad_maximum_fusion
  37.7 1.6 copy.55
  39.2 0.3 copy.56
  39.6 0.8 copy.57
  40.4 16.4 %all-to-all-start = ((bf16[128,2,2,128]{3,2,1,0:T(2,128)(2,1)}), bf16[128,2,2,128]{3,2,1,0:T(2,128)(2,1)S(1)}, u32[]{:S(2)}, u32[]{:S(2)}) async-start(bf16[128,2,2,128]{3,2,1,0:T(2,128)(2,1)} %copy.57), calls=%async_computation | async-start | bytes 262144 | tf_op jit(solution)/shard_map/all_to_all | solution.py:129
  56.8 3.8 pad_maximum_fusion.1
  60.7 0.4 copy.61
  61.1 0.1 copy.62
  61.1 8.8 all-to-all-done
  69.9 1.9 broadcast_in_dim.42
  71.8 5.9 all-to-all-start.1
  77.8 0.1 compare_and_fusion
  77.9 0.6 gather_fusion
  78.4 0.1 fusion.73
  78.5 54.0 %all-to-all-done.1 = bf16[128,2,2,16,128]{4,3,2,1,0:T(8,128)(2,1)S(1)} async-done(((bf16[128,2,2,16,128]{4,3,2,1,0:T(8,128)(2,1)}), bf16[128,2,2,16,128]{4,3,2,1,0:T(8,128)(2,1)S(1)}, u32[]{:S(2)}, u32[]{:S(2)}) %all-to-all-start.1) | async-done | bytes 2097184 | tf_op jit(solution)/shard_map/all_to_all | solution.py:130
  132.5 1.7 copy.63
  134.2 1178.5 %all-reduce.3.cloned.1.call-done = (bf16[3,256,2048]{2,1,0:T(8,128)(2,1)}, bf16[3,256,2048]{2,1,0:T(8,128)(2,1)}) async-done(((bf16[3,256,2048]{2,1,0:T(8,128)(2,1)}, bf16[3,256,2048]{2,1,0:T(8,128)(2,1)}), (bf16[3,256,2048]{2,1,0:T(8,128)(2,1)}, bf16[3,256,2048]{2,1,0:T(8,128)(2,1)})) %all-reduce.3.cloned.1.call-update) | async-done | bytes 6291472 | tf_op jit(solution)/shard_map/psum | solution.py:18
  1312.7 0.8 fusion.55
  1313.5 1.0 fusion.41
  1314.6 0.8 fusion.57
  1315.4 1.2 fusion.76
  1316.6 1.7 fusion.77
  1318.3 1.0 fusion.37
  1319.3 0.5 fusion.31
  1319.9 1.2 fusion.78
  1321.1 0.6 fusion.79
  1321.7 1.1 fusion.39
  1322.8 0.5 fusion.34
  1323.3 0.8 pad_maximum_fusion.2
  1324.2 12.3 all-to-all-start.2
  1336.5 0.1 broadcast_select_fusion
  1336.5 14.0 all-to-all-done.2
  1350.6 0.1 copy.73
  1350.6 0.1 dot_general.41
  1350.7 103.5 %all-gather.3.cloned.1.call-done = bf16[1,2048,3072]{2,1,0:T(8,128)(2,1)} async-done(((bf16[1,16,3072]{2,1,0:T(8,128)(2,1)}), bf16[1,2048,3072]{2,1,0:T(8,128)(2,1)}) %all-gather.3.cloned.1.call-update) | async-done | bytes 12582928 | tf_op jit(solution)/shard_map/all_gather | solution.py:166
  1454.2 6.8 fusion.8
  1461.1 0.4 collective-permute-start
  1461.5 0.6 maximum_bitcast_fusion.1
  1462.1 5.3 collective-permute-done
  1467.4 0.7 copy.77
  (34 shorter events, 0.4 us)
Async XLA Ops:
  7.2 70.7 %copy-start = (f32[1,4,3072]{2,1,0:T(4,128)S(1)}, f32[1,4,3072]{2,1,0:T(4,128)}, u32[]{:S(2)}) copy-start(f32[1,4,3072]{2,1,0:T(4,128)} %param.15) | copy-start | bytes 147460
  7.2 1305.5 %all-reduce.3.cloned.1.call-start = ((), (), s32[]{:S(2)}) async-start(), calls=%async_computation.4 | async-start | bytes 12582912 | tf_op jit(solution)/shard_map/psum | solution.py:18
  19.8 1.0 copy-start.2
  19.8 1.6 copy-start.5
  19.8 1434.4 %all-gather.3.cloned.1.call-start = ((), (), s32[]{:S(2)}) async-start(), calls=%async_computation.3 | async-start | bytes 12681216 | tf_op jit(solution)/shard_map/all_gather | solution.py:166
  21.7 2.7 copy-start.6
  40.4 29.5 %all-to-all-start = ((bf16[128,2,2,128]{3,2,1,0:T(2,128)(2,1)}), bf16[128,2,2,128]{3,2,1,0:T(2,128)(2,1)S(1)}, u32[]{:S(2)}, u32[]{:S(2)}) async-start(bf16[128,2,2,128]{3,2,1,0:T(2,128)(2,1)} %copy.57), calls=%async_computation | async-start | bytes 262144 | tf_op jit(solution)/shard_map/all_to_all | solution.py:129
  71.8 6.0 copy-start.4
  71.8 60.7 %all-to-all-start.1 = ((bf16[128,2,2,16,128]{4,3,2,1,0:T(8,128)(2,1)}), bf16[128,2,2,16,128]{4,3,2,1,0:T(8,128)(2,1)S(1)}, u32[]{:S(2)}, u32[]{:S(2)}) async-start(bf16[128,2,2,16,128]{4,3,2,1,0:T(8,128)(2,1)} %bitcast.145), calls=%async_computation.1 | async-start | bytes 4194304 | tf_op jit(solution)/shard_map/all_to_all | solution.py:130
  134.2 1185.1 %copy-start.1 = (bf16[128,2,2,16,128]{4,3,0,2,1:T(8,128)(2,1)S(1)}, bf16[128,2,2,16,128]{4,3,0,2,1:T(8,128)(2,1)}, u32[]{:S(2)}) copy-start(bf16[128,2,2,16,128]{4,3,0,2,1:T(8,128)(2,1)} %copy.63) | copy-start | bytes 6291460
  1321.7 132.5 %copy-start.3 = (bf16[1,2,16,3072]{3,2,1,0:T(8,128)(2,1)S(1)}, bf16[1,2,16,3072]{3,2,1,0:T(8,128)(2,1)}, u32[]{:S(2)}) copy-start(bf16[1,2,16,3072]{3,2,1,0:T(8,128)(2,1)} %param.10) | copy-start | bytes 589828
  1324.2 26.4 %all-to-all-start.2 = ((bf16[128,2,2,128]{3,2,1,0:T(2,128)(2,1)}), bf16[128,2,2,128]{3,2,1,0:T(2,128)(2,1)S(1)}, u32[]{:S(2)}, u32[]{:S(2)}) async-start(bf16[128,2,2,128]{3,2,1,0:T(2,128)(2,1)} %pad_maximum_fusion.2), calls=%async_computation.2 | async-start | bytes 262144 | tf_op jit(solution)/shard_map/all_to_all | solution.py:159
  1461.1 6.3 collective-permute-start
Sparse Core Ops, SparseCore 0:
  19.9 1292.7 all-reduce.2
  1317.2 136.9 all-gather.2
where the time goes:
time: 1480 us; the launch traced here: 1470 us
  waiting for transfers between devices  1360 us (92%)
  starting transfers between devices  35.1 us (2%)
  other arithmetic  26.4 us (2%)
  between operations  19.7 us (1%)
    psum x1, waiting for transfers between devices, from_root(): return lax.psum(block, axis)  1180 us
    all_gather x1, waiting for transfers between devices, per_device(): lax.all_gather(out_weight[0], 'seq', axis=0, tiled=True)  104 us
    all_to_all x1, waiting for transfers between devices, per_device(): lax.all_to_all(pair_send, 'seq', split_axis=0, concat_axis=0, tiled=True)  54 us
  transfers between devices with their start and end apart: 6, of which 6 were waited for; matrix products, arithmetic and copies ran while one was open for 3% of the time, Pallas kernels for 0%

commit v1 on v0

v1 whole, which is shorter than its diff:
```python
import functools
import math

import jax
import jax.numpy as jnp
import numpy as np
from jax import lax
from jax.experimental import pallas as pl
from jax.experimental.pallas import tpu as pltpu
from jax.sharding import PartitionSpec as P

COLS = 128
EPSILON = 1e-06
THETA = 10000.0
DIMS = (4, 2, 8)
CORES = 2
HEAD = 128
MESH = pl.DeviceIdType.MESH


def rope_table(tokens):
    rows = tokens // COLS
    time_dims = HEAD // 8
    space = (HEAD - time_dims) // 2
    frequency = np.exp(-math.log(THETA) * np.arange(0, space, 2) / space).astype(np.float32)

    def angles(count):
        at = np.arange(count, dtype=np.float32)[:, None] * frequency[None, :]
        return np.repeat(at.astype(np.float64), 2, axis=1)

    table = np.zeros((2, rows + COLS, HEAD), np.float32)
    sign = np.where(np.arange(space) % 2 == 0, -1.0, 1.0)
    table[0, :rows, :time_dims] = 1.0
    by_row = slice(time_dims, time_dims + space)
    by_col = slice(time_dims + space, HEAD)
    table[0, :rows, by_row] = np.cos(angles(rows))
    table[1, :rows, by_row] = np.sin(angles(rows)) * sign
    table[0, rows:, by_col] = np.cos(angles(COLS))
    table[1, rows:, by_col] = np.sin(angles(COLS)) * sign
    return table


def normalize(raw, gain):
    field = raw.astype(jnp.float32)
    return field * lax.rsqrt(jnp.mean(field * field, axis=-1, keepdims=True) + EPSILON) * gain


def drain(ref, sem):
    pltpu.make_async_copy(ref, ref, sem).wait()


def kernel(
    dims,
    owner_ref,
    plan_ref,
    gains_ref,
    table_ref,
    gate_ref,
    qkv_ref,
    hidden_ref,
    text_ref,
    weight_ref,
    handed_ref,
    text_out_ref,
    slots,
    stage1,
    recv1,
    stage2,
    recv2,
    text_q,
    text_kv,
    qkv_send,
    qkv_recv,
    image_kv,
    num,
    den,
    rows_out,
    text_send,
    attn,
    wts,
    hid,
    total,
    out_send,
    send,
    recv,
    local,
    chunk_send,
    chunk_recv,
    chunk_local,
    ring_send,
    ring_recv,
):
    nx, ny, nz = dims
    plane = ny * nz
    seq = lax.axis_index("seq")
    section = lax.axis_index("section")
    core = seq % CORES
    yz = (seq // CORES) % plane
    x = seq // (CORES * plane)
    y, z = yz // nz, yz % nz
    other = CORES - 1 - core
    block = x * CORES + core
    blocks = nx * CORES
    tokens = qkv_ref.shape[3]
    group = text_q.shape[0]
    half = group // CORES
    width = hid.shape[-1]
    inner = attn.shape[-1]
    scale = math.log2(math.e) / math.sqrt(HEAD)

    def at(x_, yz_, core_):
        return (x_ * plane + yz_) * CORES + core_

    def remote(src, dst, send_sem, recv_sem, where, section_=None):
        place = {"seq": where} if section_ is None else {"seq": where, "section": section_}
        pltpu.make_async_remote_copy(
            src_ref=src, dst_ref=dst, send_sem=send_sem, recv_sem=recv_sem,
            device_id=place, device_id_type=MESH,
        ).start()

    def lanes(index, size):
        return pl.ds(pl.multiple_of(index * size, size), size)

    barrier = pltpu.get_barrier_semaphore()

    def greet(where, section_=None):
        place = {"seq": where} if section_ is None else {"seq": where, "section": section_}
        pl.semaphore_signal(barrier, inc=1, device_id=place, device_id_type=MESH)

    here = yz * CORES + core

    @pl.loop(1, plane * CORES)
    def _(i):
        greet(x * plane * CORES + lax.rem(here + i, plane * CORES))

    for dx in range(1, nx):
        for c in range(CORES):
            greet(at((x + dx) % nx, yz, c))
    for x_ in range(nx):
        for c in range(CORES):
            greet(at(x_, yz, c), 1 - section)
    per_head = nx * CORES
    for m in range(CORES):
        source = at((seq % per_head) // CORES, seq // per_head, m)

        @pl.when(source != seq)
        def _():
            greet(source)

    text_dest = [yz * per_head + CORES * x + part for part in range(CORES)]
    to_self = sum((dest == seq).astype(jnp.int32) for dest in text_dest)
    pl.semaphore_wait(
        barrier, plane * CORES - 1 + CORES * (nx - 1) + CORES * nx + CORES - to_self
    )

    order = sorted(range(nx), key=lambda d: -min(d, nx - d))
    for i, dx in enumerate(order):
        rows = lanes((x + dx) % nx, group)
        remote(
            text_ref.at[0, other, 0, :, rows, :], slots.at[core, :, rows, :],
            chunk_send.at[i], chunk_recv.at[i], at(x, yz, other),
        )
        pltpu.make_async_copy(
            text_ref.at[0, core, 0, :, rows, :], slots.at[core, :, rows, :], chunk_local.at[i]
        ).start()

    for dx in range(nx):
        for dc in range(CORES):
            x_, c_ = (x + dx) % nx, (core + dc) % CORES
            columns = lanes(x_ * CORES + c_, width)
            weight_from, weight_to = weight_ref.at[0, :, columns], wts.at[z, y, block]
            hidden_from, hidden_to = hidden_ref.at[0, :, :, columns], hid.at[block]
            if dx == 0 and dc == 0:
                pltpu.make_async_copy(weight_from, weight_to, local.at[0]).start()
                pltpu.make_async_copy(hidden_from, hidden_to, local.at[1]).start()
            else:
                remote(weight_from, weight_to, send.at[0], recv.at[0], at(x_, yz, c_))
                remote(hidden_from, hidden_to, send.at[1], recv.at[1], at(x_, yz, c_))

    first = seq * tokens
    row_line = first // COLS
    col_line = pl.multiple_of(table_ref.shape[1] - COLS + first % COLS, tokens)
    cosine = table_ref[0, pl.ds(row_line, 1), :] + table_ref[0, pl.ds(col_line, tokens), :]
    sine = table_ref[1, pl.ds(row_line, 1), :] + table_ref[1, pl.ds(col_line, tokens), :]
    even = lax.broadcasted_iota(jnp.int32, (tokens, HEAD), 1) % 2 == 0

    @pl.loop(0, plane)
    def _(head):
        span = lanes(head, HEAD)
        for m in range(CORES):
            for t in range(2):
                field = normalize(qkv_ref[0, m, t, :, span], gains_ref[0, t, :][None, :])
                swapped = jnp.where(
                    even, pltpu.roll(field, HEAD - 1, 1), pltpu.roll(field, 1, 1)
                )
                qkv_send[head, m, t] = (field * cosine + swapped * sine).astype(jnp.bfloat16)
            qkv_send[head, m, 2] = qkv_ref[0, m, 2, :, span]
            dest = at(x, head, m)

            @pl.when(dest != seq)
            def _():
                remote(
                    qkv_send.at[head, m], qkv_recv.at[here], send.at[2], recv.at[2], dest
                )

            @pl.when(dest == seq)
            def _():
                pltpu.make_async_copy(
                    qkv_send.at[head, m], qkv_recv.at[here], local.at[2]
                ).start()

    core_of = [(owner_ref[plan_ref[section * CORES + m]]) % CORES for m in range(CORES)]
    yz_of = [(owner_ref[plan_ref[section * CORES + m]] // CORES) % plane for m in range(CORES)]
    x_of = [owner_ref[plan_ref[section * CORES + m]] // (CORES * plane) for m in range(CORES)]
    pick = lambda pair: jnp.where(core == 0, pair[0], pair[1])
    own_core, own_yz, own_x = pick(core_of), pick(yz_of), pick(x_of)

    for i, dx in enumerate(order):
        x_ = (x + dx) % nx
        rows = lanes(x_, group)
        drain(slots.at[0, :, rows, :], chunk_recv.at[i])
        drain(slots.at[0, :, rows, :], chunk_local.at[i])
        for t in range(3):

            @pl.loop(0, plane)
            def _(head):
                span = lanes(head, HEAD)
                piece = jnp.where(own_core == 0, slots[0, t, rows, span], slots[1, t, rows, span])
                if dx == 0:
                    recv1[x, t, :, span] = piece
                else:
                    stage1[i, t, :, span] = piece

        if dx != 0:
            remote(stage1.at[i], recv1.at[x], send.at[3], recv.at[3], at(x_, yz, core))

    drain(qkv_recv.at[pl.ds(0, plane * CORES - 1)], recv.at[2])
    drain(qkv_recv.at[0], local.at[2])
    for dx in range(1, nx):
        remote(
            qkv_recv.at[:, pl.ds(1, 2)], image_kv.at[x], send.at[4], recv.at[4],
            at((x + dx) % nx, yz, core),
        )
    pltpu.make_async_copy(qkv_recv.at[:, pl.ds(1, 2)], image_kv.at[x], local.at[4]).start()

    drain(wts.at[0, 0, 0], local.at[0])
    drain(wts.at[0, 0, pl.ds(0, blocks - 1)], recv.at[0])
    for dy in range(1, ny):
        remote(
            wts.at[z, y], wts.at[z, y], send.at[7], recv.at[7],
            at(x, lax.rem(y + dy, ny) * nz + z, core),
        )
    drain(wts.at[0, pl.ds(0, ny - 1)], recv.at[7])

    steps = (nz // 2, (nz - 1) // 2)
    for step in range(steps[0]):
        for way, sign in enumerate((1, -1)):
            if step < steps[way]:
                slot = lax.rem(z - sign * step + nz, nz)
                remote(
                    wts.at[slot], wts.at[slot], ring_send.at[way, step],
                    ring_recv.at[way, step], at(x, y * nz + lax.rem(z + sign + nz, nz), core),
                )
        for way in range(2):
            if step < steps[way]:
                drain(wts.at[0], ring_recv.at[way, step])

    drain(recv1.at[pl.ds(0, nx - 1)], recv.at[3])

    @pl.loop(0, plane)
    def _(head):
        piece = recv1[own_x, :, :, lanes(head, HEAD)]
        stage2[head] = piece

        @pl.when(head == yz)
        def _():
            recv2[head] = piece

        @pl.when(head != yz)
        def _():
            remote(stage2.at[head], recv2.at[yz], send.at[5], recv.at[5], at(x, head, core))

    def meet(queries, keys, values):
        scores = lax.dot_general(
            queries, keys, (((1,), (1,)), ((), ())), preferred_element_type=jnp.float32
        )
        weights = jnp.exp2(scores * scale)
        part = weights[:, :HEAD]
        for k in range(1, keys.shape[0] // HEAD):
            part = part + weights[:, k * HEAD : (k + 1) * HEAD]
        return (
            jnp.dot(weights.astype(jnp.bfloat16), values, preferred_element_type=jnp.float32),
            part,
        )

    image_rows = plane * CORES * tokens
    row_block = HEAD
    sources = row_block // tokens

    def image_queries(index):
        return qkv_recv[pl.ds(index * sources, sources), 0].reshape(row_block, HEAD)

    def image_pair(x_):
        return [image_kv[x_, :, t].reshape(image_rows, HEAD) for t in range(2)]

    drain(image_kv.at[pl.ds(0, nx - 1)], recv.at[4])
    drain(image_kv.at[0], local.at[4])

    @pl.loop(0, image_rows // row_block)
    def _(index):
        queries = image_queries(index)
        parts = [meet(queries, *image_pair(x_)) for x_ in range(nx)]
        rows = lanes(index, row_block)
        num[rows, :] = sum(p[0] for p in parts[1:]) + parts[0][0]
        den[rows, :] = sum(p[1] for p in parts[1:]) + parts[0][1]

    drain(recv2.at[pl.ds(0, plane - 1)], recv.at[5])
    text_q[...] = normalize(recv2[own_yz, 0], gains_ref[0, 2, :][None, :]).astype(jnp.bfloat16)
    text_kv[x, 0] = normalize(recv2[own_yz, 1], gains_ref[0, 3, :][None, :]).astype(
        jnp.bfloat16
    )
    text_kv[x, 1] = recv2[own_yz, 2]
    for dx in range(1, nx):
        remote(
            text_kv.at[x], text_kv.at[x], send.at[6], recv.at[6], at((x + dx) % nx, yz, core)
        )
    queries = text_q[...]
    text_parts = [meet(queries, *image_pair(x_)) for x_ in range(nx)]
    drain(text_kv.at[pl.ds(0, nx - 1)], recv.at[6])
    text_pair = [text_kv[:, t].reshape(nx * group, HEAD) for t in range(2)]
    text_parts.append(meet(queries, *text_pair))

    def quotient(numerator, denominator):
        return (numerator / jnp.sum(denominator, axis=-1, keepdims=True)).astype(jnp.bfloat16)

    @pl.loop(0, image_rows // row_block)
    def _(index):
        rows = lanes(index, row_block)
        pair = [text_kv[:, t].reshape(nx * group, HEAD) for t in range(2)]
        more = meet(image_queries(index), *pair)
        rows_out[rows, :] = quotient(num[rows, :] + more[0], den[rows, :] + more[1])

    pair_rows = CORES * tokens
    own_lanes = lanes(yz, HEAD)

    @pl.loop(1, plane)
    def _(i):
        there = lax.rem(yz + i, plane)
        remote(
            rows_out.at[lanes(there, pair_rows), :], attn.at[block, :, own_lanes],
            send.at[9], recv.at[9], at(x, there, core),
        )

    attn[block, :, own_lanes] = rows_out[lanes(yz, pair_rows), :]

    text_rows = quotient(
        sum(p[0] for p in text_parts[1:]) + text_parts[0][0],
        sum(p[1] for p in text_parts[1:]) + text_parts[0][1],
    )
    for part, dest in enumerate(text_dest):
        text_send[part] = text_rows[part * half : (part + 1) * half, :]

        @pl.when(dest != seq)
        def _():
            remote(
                text_send.at[part], text_out_ref.at[0, 0, core], send.at[8], recv.at[8], dest
            )

        @pl.when(dest == seq)
        def _():
            pltpu.make_async_copy(
                text_send.at[part], text_out_ref.at[0, 0, core], local.at[8]
            ).start()

    drain(rows_out.at[pl.ds(0, (plane - 1) * pair_rows), :], recv.at[9])
    for dx in range(nx):
        for dc in range(CORES):
            if dx or dc:
                remote(
                    attn.at[block], attn.at[block], send.at[10], recv.at[10],
                    at((x + dx) % nx, yz, (core + dc) % CORES),
                )
    drain(attn.at[pl.ds(0, blocks - 1)], recv.at[10])

    depth = inner // (nx * ny)
    total[...] = jnp.zeros_like(total)

    @pl.loop(0, nx * ny)
    def _(k):
        left = attn[:, :, lanes(k, depth)].reshape(blocks * pair_rows, depth)
        right = wts[:, k % ny, pl.ds((k // ny) * CORES, CORES)].reshape(depth, width)
        total[...] += jnp.dot(left, right, preferred_element_type=jnp.float32)

    drain(hid.at[0], local.at[1])
    drain(hid.at[pl.ds(0, blocks - 1)], recv.at[1])
    columns = lanes(block, width)

    @pl.loop(0, blocks)
    def _(dest):
        x_, c_ = dest // CORES, dest % CORES
        for m in range(CORES):
            gate_row = gate_ref[0, pl.ds(plan_ref[section * CORES + m], 1), columns]
            rows = lanes((x_ * CORES + m) * CORES + c_, tokens)
            out_send[dest, m] = (
                hid[dest, m].astype(jnp.float32) + gate_row * total[rows, :]
            ).astype(jnp.bfloat16)
        remote(
            out_send.at[dest], handed_ref.at[0, :, :, columns], send.at[11], recv.at[11],
            at(x_, yz, c_), 1 - section,
        )

    drain(out_send, recv.at[11])

    @pl.when(to_self == 0)
    def _():
        drain(text_send, recv.at[8])
        drain(text_send, send.at[8])

    @pl.when(to_self != 0)
    def _():
        drain(text_send.at[0], recv.at[8])
        drain(text_send.at[0], local.at[8])
        drain(text_send.at[0], send.at[8])

    for i in range(nx):
        drain(slots.at[0, :, pl.ds(0, group), :], chunk_send.at[i])
    for step in range(steps[0]):
        for way in range(2):
            if step < steps[way]:
                drain(wts.at[0], ring_send.at[way, step])
    drain(wts.at[0, 0, pl.ds(0, blocks - 1)], send.at[0])
    drain(hid.at[pl.ds(0, blocks - 1)], send.at[1])
    drain(qkv_recv.at[pl.ds(0, plane * CORES - 1)], send.at[2])
    drain(recv1.at[pl.ds(0, nx - 1)], send.at[3])
    drain(image_kv.at[pl.ds(0, nx - 1)], send.at[4])
    drain(recv2.at[pl.ds(0, plane - 1)], send.at[5])
    drain(text_kv.at[pl.ds(0, nx - 1)], send.at[6])
    drain(wts.at[0, pl.ds(0, ny - 1)], send.at[7])
    drain(rows_out.at[pl.ds(0, (plane - 1) * pair_rows), :], send.at[9])
    drain(attn.at[pl.ds(0, blocks - 1)], send.at[10])
    drain(out_send, send.at[11])


def per_device(hidden, image_qkv, text_slots, norm_gains, out_weight, gate, owner, plan):
    nx, ny, nz = DIMS
    plane = ny * nz
    blocks = nx * CORES
    tokens, model = hidden.shape[2:]
    inner = image_qkv.shape[-1]
    text_len = text_slots.shape[4]
    group = text_len // nx
    width = model // blocks
    weight_rows = out_weight.shape[1]
    image_rows = plane * CORES * tokens
    table = jnp.asarray(rope_table(tokens * blocks * plane))
    bf16, f32 = jnp.bfloat16, jnp.float32
    vmem = pl.BlockSpec(memory_space=pltpu.VMEM)
    smem = pl.BlockSpec(memory_space=pltpu.SMEM)
    anywhere = pl.BlockSpec(memory_space=pl.ANY)
    dma = pltpu.SemaphoreType.DMA
    return pl.pallas_call(
        functools.partial(kernel, DIMS),
        out_shape=(
            jax.ShapeDtypeStruct(hidden.shape, bf16),
            jax.ShapeDtypeStruct((1, 1, CORES, group // CORES, HEAD), bf16),
        ),
        in_specs=[smem, smem, vmem, vmem, vmem, vmem, anywhere, anywhere, anywhere],
        out_specs=(anywhere, anywhere),
        scratch_shapes=[
            pltpu.VMEM((CORES, 3, text_len, inner), bf16),
            pltpu.VMEM((nx - 1, 3, group, inner), bf16),
            pltpu.VMEM((nx, 3, group, inner), bf16),
            pltpu.VMEM((plane, 3, group, HEAD), bf16),
            pltpu.VMEM((plane, 3, group, HEAD), bf16),
            pltpu.VMEM((group, HEAD), bf16),
            pltpu.VMEM((nx, 2, group, HEAD), bf16),
            pltpu.VMEM((plane, CORES, 3, tokens, HEAD), bf16),
            pltpu.VMEM((plane * CORES, 3, tokens, HEAD), bf16),
            pltpu.VMEM((nx, plane * CORES, 2, tokens, HEAD), bf16),
            pltpu.VMEM((image_rows, HEAD), f32),
            pltpu.VMEM((image_rows, HEAD), f32),
            pltpu.VMEM((image_rows, HEAD), bf16),
            pltpu.VMEM((CORES, group // CORES, HEAD), bf16),
            pltpu.VMEM((blocks, CORES * tokens, inner), bf16),
            pltpu.VMEM((nz, ny, blocks, weight_rows, width), bf16),
            pltpu.VMEM((blocks, CORES, tokens, width), bf16),
            pltpu.VMEM((blocks * CORES * tokens, width), f32),
            pltpu.VMEM((blocks, CORES, tokens, width), bf16),
            dma((12,)),
            dma((12,)),
            dma((12,)),
            dma((nx,)),
            dma((nx,)),
            dma((nx,)),
            dma((2, nz // 2)),
            dma((2, nz // 2)),
        ],
        compiler_params=pltpu.CompilerParams(
            collective_id=0, has_side_effects=True, vmem_limit_bytes=48 * 2**20
        ),
    )(
        owner,
        plan,
        norm_gains,
        table,
        gate,
        image_qkv.transpose(0, 1, 3, 2, 4),
        hidden,
        text_slots,
        out_weight,
    )


def solution(mesh):
    return jax.shard_map(
        per_device,
        mesh=mesh,
        in_specs=(
            P("section", None, "seq", None),
            P("section", None, "seq", None, None),
            P("section", None, "seq", None, None, None),
            P("section", None, None),
            P("section", "seq", None),
            P("section", None, None),
            P(),
            P(),
        ),
        out_specs=(P("section", None, "seq", None), P("section", "seq", None, None, None)),
        check_vma=False,
    )
```

time: 1480 us -> 117 us (0.08)
  waiting for transfers between devices: 1360 us -> 0 us
  Pallas kernels: 0 us -> 108 us
  starting transfers between devices: 35.1 us -> 0 us
  other arithmetic: 26.4 us -> 0 us
  between operations: 19.7 us -> 0.66 us
    psum x1 -> x0, waiting for transfers between devices: 1180 us -> none  [from_root(): return lax.psum(block, axis)]
    pallas_call x0 -> x1, Pallas kernels: none -> 108 us  [per_device(): pl.pallas_call(functools.partial(kernel, DIMS), out_shape=(jax.ShapeDtype...]
    all_gather x1 -> x0, waiting for transfers between devices: 104 us -> none  [per_device(): lax.all_gather(out_weight[0], 'seq', axis=0, tiled=True)]
    all_to_all x3 -> x0, waiting for transfers between devices: 76.8 us -> none  [the longest x1 54 us: per_device(): lax.all_to_all(pair_send, 'seq', split_axis=0, concat_axis=0, tiled=True)]
    all_to_all x3 -> x0, starting transfers between devices: 34.6 us -> none  [the longest x1 16.4 us: per_device(): lax.all_to_all(query_send, 'seq', split_axis=0, concat_axis=0, tiled=True)]
  transfers between devices with their start and end apart: 6 -> 0, of which waited for: 6 -> 0; matrix products, arithmetic and copies ran while one was open for 3% -> 0% of each run, Pallas kernels for 0% -> 0%
where the time goes in v1:
time: 117 us
  Pallas kernels  108 us (92%)
  local copies, waits for them, and re-layouts  7.79 us (7%)
    pallas_call x1, Pallas kernels, per_device(): pl.pallas_call(functools.partial(kernel, DIMS), out_shape=(jax.ShapeDtype...  108 us
    unnamed x18, local copies, waits for them, and re-layouts  7.79 us

profile of v1, /device:TPU:1, one launch (start us, length us, event | category | flops | bytes accessed | tf_op | source)
XLA Modules:
  0.0 116.7 jit_solution(1561816769807126555)
XLA Ops:
  0.6 0.0 copy-start
  0.6 1.0 copy-done
  1.6 0.0 copy-start.1
  1.6 0.9 copy-done.1
  2.6 0.0 copy-start.2
  2.6 0.9 copy-done.2
  3.5 0.0 copy-start.3
  3.5 0.9 copy-done.3
  4.4 0.0 copy-start.4
  4.4 0.8 copy-done.4
  5.2 0.0 copy-start.5
  5.2 0.7 copy-done.5
  5.8 0.0 copy-start.6
  5.8 0.7 copy-done.6
  6.5 0.0 copy-start.7
  6.5 0.7 copy-done.7
  7.2 108.2 %shard_map.104 = (bf16[1,2,16,3072]{3,2,1,0:T(8,128)(2,1)S(1)}, bf16[1,1,2,32,128]{4,3,2,1,0:T(8,128)(2,1)S(1)}) custom-call(s32[4]{0:T(128)S(1)} %copy-done.6, s32[4]{0:T(128)S(1)} %copy-done.7, f32[1,4,128]{2,1,0:T(4,128)S(1)} %copy-done.5, f32[2,144,128]{2,1,0:T(8,128)S(1)} %copy-done.2, f32[1,4,3072]{2,1,0:T(4,128)S(1)} %copy-done.4, ...), custom_call_target="tpu_custom_call" | custom-call | tf_op jit(solution)/shard_map/pallas_call | solution.py:461
  115.4 0.7 copy.13
  116.1 0.6 copy.14
Async XLA Ops:
  0.6 1.0 copy-start
  1.6 0.9 copy-start.1
  2.6 0.9 copy-start.2
  3.5 0.9 copy-start.3
  4.4 0.8 copy-start.4
  5.2 0.7 copy-start.5
  5.8 0.7 copy-start.6
  6.5 0.7 copy-start.7

commit v2 on v1

v2 whole, which is shorter than its diff:
```python
import functools
import math

import jax
import jax.numpy as jnp
import numpy as np
from jax import lax
from jax.experimental import pallas as pl
from jax.experimental.pallas import tpu as pltpu
from jax.sharding import PartitionSpec as P

COLS = 128
EPSILON = 1e-06
THETA = 10000.0
DIMS = (4, 2, 8)
CORES = 2
HEAD = 128
MESH = pl.DeviceIdType.MESH


def rope_table(tokens):
    rows = tokens // COLS
    time_dims = HEAD // 8
    space = (HEAD - time_dims) // 2
    frequency = np.exp(-math.log(THETA) * np.arange(0, space, 2) / space).astype(np.float32)

    def angles(count):
        at = np.arange(count, dtype=np.float32)[:, None] * frequency[None, :]
        return np.repeat(at.astype(np.float64), 2, axis=1)

    table = np.zeros((2, rows + COLS, HEAD), np.float32)
    sign = np.where(np.arange(space) % 2 == 0, -1.0, 1.0)
    table[0, :rows, :time_dims] = 1.0
    by_row = slice(time_dims, time_dims + space)
    by_col = slice(time_dims + space, HEAD)
    table[0, :rows, by_row] = np.cos(angles(rows))
    table[1, :rows, by_row] = np.sin(angles(rows)) * sign
    table[0, rows:, by_col] = np.cos(angles(COLS))
    table[1, rows:, by_col] = np.sin(angles(COLS)) * sign
    return table


def normalize(raw, gain):
    field = raw.astype(jnp.float32)
    return field * lax.rsqrt(jnp.mean(field * field, axis=-1, keepdims=True) + EPSILON) * gain


def drain(ref, sem):
    pltpu.make_async_copy(ref, ref, sem).wait()


def kernel(
    dims,
    owner_hbm,
    plan_hbm,
    gains_hbm,
    table_hbm,
    gate_hbm,
    qkv_hbm,
    hidden_ref,
    text_ref,
    weight_ref,
    handed_ref,
    text_out_ref,
    owner_ref,
    plan_ref,
    gains_ref,
    table_ref,
    gate_ref,
    qkv_ref,
    slots,
    a1_out,
    a1_0,
    a1_1,
    a1_2,
    a2_out,
    a2_0,
    a2_1,
    a2_2,
    b1_out,
    b1_0,
    b1_1,
    b1_2,
    b2_out,
    b2_0,
    b2_1,
    b2_2,
    z_out,
    z_in_0,
    z_in_1,
    z_in_2,
    text_q,
    text_kv,
    qkv_send,
    qkv_recv,
    image_kv,
    num,
    den,
    rows_out,
    text_send,
    attn,
    wts,
    hid,
    total,
    out_send,
    send,
    recv,
    local,
    t_send,
    t_recv,
    t_local,
    ring_send,
    ring_recv,
    line_recv,
):
    nx, ny, nz = dims
    plane = ny * nz
    seq = lax.axis_index("seq")
    section = lax.axis_index("section")
    core = seq % CORES
    yz = (seq // CORES) % plane
    x = seq // (CORES * plane)
    y, z = yz // nz, yz % nz
    other = CORES - 1 - core
    far = ny - 1 - y
    block = x * CORES + core
    blocks = nx * CORES
    here = yz * CORES + core
    tokens = qkv_ref.shape[2]
    group = text_q.shape[0]
    half = group // CORES
    a1, a2, b1, b2 = (a1_0, a1_1, a1_2), (a2_0, a2_1, a2_2), (b1_0, b1_1, b1_2), (b2_0, b2_1, b2_2)
    z_in = z_in_0, z_in_1, z_in_2
    rows_a, rows_b, wide = a1_0.shape[1], b1_0.shape[2], b1_0.shape[3]
    width = hid.shape[-1]
    inner = attn.shape[-1]
    scale = math.log2(math.e) / math.sqrt(HEAD)

    def at(x_, yz_, core_):
        return (x_ * plane + yz_) * CORES + core_

    def remote(src, dst, send_sem, recv_sem, where, section_=None):
        place = {"seq": where} if section_ is None else {"seq": where, "section": section_}
        pltpu.make_async_remote_copy(
            src_ref=src, dst_ref=dst, send_sem=send_sem, recv_sem=recv_sem,
            device_id=place, device_id_type=MESH,
        ).start()

    def lanes(index, size):
        return pl.ds(pl.multiple_of(index * size, size), size)

    loads = [
        (qkv_hbm.at[0], qkv_ref),
        (table_hbm, table_ref),
        (gains_hbm.at[0], gains_ref),
        (owner_hbm, owner_ref),
        (plan_hbm, plan_ref),
        (gate_hbm.at[0], gate_ref),
    ]
    loads = [
        pltpu.make_async_copy(src, dst, local.at[3 + i]) for i, (src, dst) in enumerate(loads)
    ]
    for load in loads:
        load.start()

    barrier = pltpu.get_barrier_semaphore()

    def greet(where, section_=None):
        place = {"seq": where} if section_ is None else {"seq": where, "section": section_}
        pl.semaphore_signal(barrier, inc=1, device_id=place, device_id_type=MESH)

    @pl.loop(1, plane * CORES)
    def _(i):
        greet(x * plane * CORES + lax.rem(here + i, plane * CORES))

    for dx in range(1, nx):
        for c in range(CORES):
            greet(at((x + dx) % nx, yz, c))
    for x_ in range(nx):
        for c in range(CORES):
            greet(at(x_, yz, c), 1 - section)
    per_head = nx * CORES
    for m in range(CORES):
        source = at((seq % per_head) // CORES, seq // per_head, m)

        @pl.when(source != seq)
        def _():
            greet(source)

    text_dest = [yz * per_head + CORES * x + part for part in range(CORES)]
    to_self = sum((dest == seq).astype(jnp.int32) for dest in text_dest)

    for load in loads:
        load.wait()
    own = owner_ref[plan_ref[section * CORES + core]]
    own_core, own_yz, own_x = own % CORES, (own // CORES) % plane, own // (CORES * plane)
    own_y, own_z = own_yz // nz, own_yz % nz

    pl.semaphore_wait(
        barrier, plane * CORES - 1 + CORES * (nx - 1) + CORES * nx + CORES - to_self
    )

    order = (1, 2, 0)
    for t in order:
        remote(
            text_ref.at[0, other, 0, t], slots.at[core, t], t_send.at[0, t], t_recv.at[0, t],
            at(x, yz, other),
        )
        pltpu.make_async_copy(
            text_ref.at[0, core, 0, t], slots.at[core, t], t_local.at[t]
        ).start()

    def spread(t):
        drain(slots.at[0, t], t_recv.at[0, t])
        drain(slots.at[0, t], t_local.at[t])

        def fill(dst, row, count, lane, size):
            chunk = min(size, 512)

            @pl.loop(0, size // chunk)
            def _(k):
                span = pl.ds(pl.multiple_of(lane + k * chunk, HEAD), chunk)
                rows = pl.ds(pl.multiple_of(row, 16), count)
                dst[:, lanes(k, chunk)] = jnp.where(
                    own_core == 0, slots[0, t, rows, span], slots[1, t, rows, span]
                )

        for dx in sorted(range(nx), key=lambda d: -min(d, nx - d)):
            x_ = (x + dx) % nx
            if dx == 0:
                fill(a1[t].at[x], x_ * group, rows_a, 0, inner)
            else:
                fill(a1_out.at[t, dx - 1], x_ * group, rows_a, 0, inner)
                remote(
                    a1_out.at[t, dx - 1], a1[t].at[x], t_send.at[1, t], t_recv.at[1, t],
                    at(x_, yz, core),
                )

        @pl.loop(0, nx)
        def _(g):
            fill(b1_out.at[t, g], g * group + rows_a, rows_b, far * wide, wide)
            fill(b1[t].at[y, g], g * group + rows_a, rows_b, y * wide, wide)

        remote(
            b1_out.at[t], b1[t].at[y], t_send.at[2, t], t_recv.at[2, t],
            at(x, far * nz + z, core),
        )

    def cross(t):
        drain(a1[t].at[pl.ds(0, nx - 1)], t_recv.at[1, t])
        a2_out[t] = a1[t][own_x, :, lanes(far, wide)]
        remote(
            a2_out.at[t], a2[t].at[y], t_send.at[3, t], t_recv.at[3, t],
            at(x, far * nz + z, core),
        )
        a2[t][y] = a1[t][own_x, :, lanes(y, wide)]
        drain(b1[t].at[0], t_recv.at[2, t])
        for dx in sorted(range(nx), key=lambda d: -min(d, nx - d)):
            x_ = (x + dx) % nx
            if dx == 0:
                b2[t][x] = b1[t][own_y, x_]
            else:
                b2_out[t, dx - 1] = b1[t][own_y, x_]
                remote(
                    b2_out.at[t, dx - 1], b2[t].at[x], t_send.at[4, t], t_recv.at[4, t],
                    at(x_, yz, core),
                )

    def deal(t):
        drain(a2[t].at[0], t_recv.at[3, t])
        drain(b2[t].at[pl.ds(0, nx - 1)], t_recv.at[4, t])

        def fill(dst, z_):
            dst[pl.ds(0, rows_a), :] = a2[t][own_y, :, lanes(z_, HEAD)]
            dst[pl.ds(rows_a, rows_b), :] = b2[t][own_x, :, lanes(z_, HEAD)]

        fill(z_in[t].at[z], z)

        @pl.loop(1, nz)
        def _(dz):
            z_ = lax.rem(z + dz, nz)
            fill(z_out.at[t, z_], z_)
            remote(
                z_out.at[t, z_], z_in[t].at[z], t_send.at[5, t], t_recv.at[5, t],
                at(x, y * nz + z_, core),
            )

    def weights_start():
        for dx in range(nx):
            for dc in range(CORES):
                x_, c_ = (x + dx) % nx, (core + dc) % CORES
                columns = lanes(x_ * CORES + c_, width)
                weight_from, weight_to = weight_ref.at[0, :, columns], wts.at[z, y, block]
                if dx == 0 and dc == 0:
                    pltpu.make_async_copy(weight_from, weight_to, local.at[0]).start()
                else:
                    remote(weight_from, weight_to, send.at[0], recv.at[0], at(x_, yz, c_))

    def hidden_start():
        for dx in range(nx):
            for dc in range(CORES):
                x_, c_ = (x + dx) % nx, (core + dc) % CORES
                columns = lanes(x_ * CORES + c_, width)
                hidden_from, hidden_to = hidden_ref.at[0, :, :, columns], hid.at[block]
                if dx == 0 and dc == 0:
                    pltpu.make_async_copy(hidden_from, hidden_to, local.at[1]).start()
                else:
                    remote(hidden_from, hidden_to, send.at[1], recv.at[1], at(x_, yz, c_))

    def weights_over_y():
        drain(wts.at[0, 0, 0], local.at[0])
        drain(wts.at[0, 0, pl.ds(0, blocks - 1)], recv.at[0])
        remote(wts.at[z, y], wts.at[z, y], send.at[7], recv.at[7], at(x, far * nz + z, core))

    steps = (nz // 2, (nz - 1) // 2)

    def ring(step):
        if step == 0:
            drain(wts.at[0, 0], recv.at[7])
        for way, sign in enumerate((1, -1)):
            if 0 < step <= steps[way]:
                drain(wts.at[0], ring_recv.at[way, step - 1])
            if step < steps[way]:
                slot = lax.rem(z - sign * step + nz, nz)
                remote(
                    wts.at[slot], wts.at[slot], ring_send.at[way, step],
                    ring_recv.at[way, step], at(x, y * nz + lax.rem(z + sign + nz, nz), core),
                )

    def heads_start():
        @pl.loop(0, plane)
        def _(head):
            for m in range(CORES):
                dest = at(x, head, m)

                @pl.when(dest != seq)
                def _():
                    remote(
                        qkv_send.at[head, m], qkv_recv.at[here], send.at[2], recv.at[2], dest
                    )

                @pl.when(dest == seq)
                def _():
                    pltpu.make_async_copy(
                        qkv_send.at[head, m], qkv_recv.at[here], local.at[2]
                    ).start()

    def keys_start():
        drain(qkv_recv.at[pl.ds(0, plane * CORES - 1)], recv.at[2])
        drain(qkv_recv.at[0], local.at[2])
        for dx in range(1, nx):
            remote(
                qkv_recv.at[:, pl.ds(1, 2)], image_kv.at[x], send.at[4], recv.at[4],
                at((x + dx) % nx, yz, core),
            )
        pltpu.make_async_copy(
            qkv_recv.at[:, pl.ds(1, 2)], image_kv.at[x], local.at[2]
        ).start()

    weights_start()
    spread(order[0])
    first = seq * tokens
    row_line = first // COLS
    col_line = pl.multiple_of(table_ref.shape[1] - COLS + first % COLS, tokens)
    cosine = table_ref[0, pl.ds(row_line, 1), :] + table_ref[0, pl.ds(col_line, tokens), :]
    sine = table_ref[1, pl.ds(row_line, 1), :] + table_ref[1, pl.ds(col_line, tokens), :]
    even = lax.broadcasted_iota(jnp.int32, (tokens, HEAD), 1) % 2 == 0

    @pl.loop(0, plane)
    def _(head):
        span = lanes(head, HEAD)
        for m in range(CORES):
            for t in range(2):
                field = normalize(qkv_ref[m, t, :, span], gains_ref[t, :][None, :])
                swapped = jnp.where(
                    even, pltpu.roll(field, HEAD - 1, 1), pltpu.roll(field, 1, 1)
                )
                qkv_send[head, m, t] = (field * cosine + swapped * sine).astype(jnp.bfloat16)
            qkv_send[head, m, 2] = qkv_ref[m, 2, :, span]

    heads_start()
    weights_over_y()
    spread(order[1])
    spread(order[2])
    ring(0)
    cross(order[0])
    ring(1)
    cross(order[1])
    ring(2)
    deal(order[0])
    cross(order[2])
    ring(3)
    keys_start()
    deal(order[1])
    deal(order[2])
    hidden_start()
    for step in range(4, steps[0] + 1):
        ring(step)

    def meet(queries, keys, values):
        scores = lax.dot_general(
            queries, keys, (((1,), (1,)), ((), ())), preferred_element_type=jnp.float32
        )
        weights = jnp.exp2(scores * scale)
        part = weights[:, :HEAD]
        for k in range(1, keys.shape[0] // HEAD):
            part = part + weights[:, k * HEAD : (k + 1) * HEAD]
        return (
            jnp.dot(weights.astype(jnp.bfloat16), values, preferred_element_type=jnp.float32),
            part,
        )

    image_rows = plane * CORES * tokens
    row_block = HEAD
    sources = row_block // tokens

    def image_queries(index):
        return qkv_recv[pl.ds(index * sources, sources), 0].reshape(row_block, HEAD)

    def image_pair(x_):
        return [image_kv[x_, :, t].reshape(image_rows, HEAD) for t in range(2)]

    drain(image_kv.at[pl.ds(0, nx - 1)], recv.at[4])
    drain(image_kv.at[0], local.at[2])

    @pl.loop(0, image_rows // row_block)
    def _(index):
        queries = image_queries(index)
        parts = [meet(queries, *image_pair(x_)) for x_ in range(nx)]
        rows = lanes(index, row_block)
        num[rows, :] = sum(p[0] for p in parts[1:]) + parts[0][0]
        den[rows, :] = sum(p[1] for p in parts[1:]) + parts[0][1]

    def text_rows_of(t):
        drain(z_in[t].at[pl.ds(0, nz - 1)], t_recv.at[5, t])
        return z_in[t][own_z]

    text_kv[x, 0] = normalize(text_rows_of(1), gains_ref[3, :][None, :]).astype(jnp.bfloat16)
    text_kv[x, 1] = text_rows_of(2)
    for dx in range(1, nx):
        remote(
            text_kv.at[x], text_kv.at[x], send.at[6], recv.at[6], at((x + dx) % nx, yz, core)
        )
    text_q[...] = normalize(text_rows_of(0), gains_ref[2, :][None, :]).astype(jnp.bfloat16)
    queries = text_q[...]
    text_parts = [meet(queries, *image_pair(x_)) for x_ in range(nx)]
    drain(text_kv.at[pl.ds(0, nx - 1)], recv.at[6])

    def quotient(numerator, denominator):
        return (numerator / jnp.sum(denominator, axis=-1, keepdims=True)).astype(jnp.bfloat16)

    pair_rows = CORES * tokens
    own_lanes = lanes(yz, HEAD)

    @pl.loop(0, image_rows // row_block)
    def _(index):
        rows = lanes(index, row_block)
        pair = [text_kv[:, t].reshape(nx * group, HEAD) for t in range(2)]
        more = meet(image_queries(index), *pair)
        rows_out[rows, :] = quotient(num[rows, :] + more[0], den[rows, :] + more[1])
        for k in range(row_block // pair_rows):
            there = index * (row_block // pair_rows) + k

            @pl.when(there != yz)
            def _():
                remote(
                    rows_out.at[lanes(there, pair_rows), :], attn.at[x, core, :, own_lanes],
                    send.at[9], recv.at[9], at(x, there, core),
                )

    attn[x, core, :, own_lanes] = rows_out[lanes(yz, pair_rows), :]

    text_pair = [text_kv[:, t].reshape(nx * group, HEAD) for t in range(2)]
    text_parts.append(meet(queries, *text_pair))
    text_rows = quotient(
        sum(p[0] for p in text_parts[1:]) + text_parts[0][0],
        sum(p[1] for p in text_parts[1:]) + text_parts[0][1],
    )
    for part, dest in enumerate(text_dest):
        text_send[part] = text_rows[part * half : (part + 1) * half, :]

        @pl.when(dest != seq)
        def _():
            remote(
                text_send.at[part], text_out_ref.at[0, 0, core], send.at[8], recv.at[8], dest
            )

        @pl.when(dest == seq)
        def _():
            pltpu.make_async_copy(
                text_send.at[part], text_out_ref.at[0, 0, core], local.at[0]
            ).start()

    drain(rows_out.at[pl.ds(0, (plane - 1) * pair_rows), :], recv.at[9])
    for dx in range(1, nx):
        remote(
            attn.at[x, core], attn.at[x, core], send.at[10], line_recv.at[0, dx],
            at((x + dx) % nx, yz, core),
        )
    remote(
        attn.at[x, core], attn.at[x, core], send.at[3], line_recv.at[1, 0], at(x, yz, other)
    )
    for dx in sorted(range(1, nx), key=lambda d: min(d, nx - d)):
        x_ = (x - dx + nx) % nx
        drain(attn.at[0, 0], line_recv.at[0, dx])
        remote(
            attn.at[x_, core], attn.at[x_, core], send.at[3], line_recv.at[1, dx],
            at(x, yz, other),
        )
    for dx in range(nx):
        drain(attn.at[0, 0], line_recv.at[1, dx])

    depth = inner // (nx * ny)
    total[...] = jnp.zeros_like(total)

    @pl.loop(0, nx * ny)
    def _(k):
        left = attn[:, :, :, lanes(k, depth)].reshape(blocks * pair_rows, depth)
        right = wts[:, k % ny, pl.ds((k // ny) * CORES, CORES)].reshape(depth, width)
        total[...] += jnp.dot(left, right, preferred_element_type=jnp.float32)

    drain(hid.at[0], local.at[1])
    drain(hid.at[pl.ds(0, blocks - 1)], recv.at[1])
    columns = lanes(block, width)

    @pl.loop(0, blocks)
    def _(dest):
        x_, c_ = dest // CORES, dest % CORES
        for m in range(CORES):
            gate_row = gate_ref[pl.ds(plan_ref[section * CORES + m], 1), columns]
            rows = lanes((x_ * CORES + m) * CORES + c_, tokens)
            out_send[dest, m] = (
                hid[dest, m].astype(jnp.float32) + gate_row * total[rows, :]
            ).astype(jnp.bfloat16)
        remote(
            out_send.at[dest], handed_ref.at[0, :, :, columns], send.at[11], recv.at[11],
            at(x_, yz, c_), 1 - section,
        )

    for t in range(3):
        drain(slots.at[0, t], t_send.at[0, t])
        drain(a1[t].at[pl.ds(0, nx - 1)], t_send.at[1, t])
        drain(b1[t].at[0], t_send.at[2, t])
        drain(a2[t].at[0], t_send.at[3, t])
        drain(b2[t].at[pl.ds(0, nx - 1)], t_send.at[4, t])
        drain(z_in[t].at[pl.ds(0, nz - 1)], t_send.at[5, t])
    for step in range(steps[0]):
        for way in range(2):
            if step < steps[way]:
                drain(wts.at[0], ring_send.at[way, step])
    drain(wts.at[0, 0, pl.ds(0, blocks - 1)], send.at[0])
    drain(hid.at[pl.ds(0, blocks - 1)], send.at[1])
    drain(qkv_recv.at[pl.ds(0, plane * CORES - 1)], send.at[2])
    drain(attn.at[:, 0], send.at[3])
    drain(image_kv.at[pl.ds(0, nx - 1)], send.at[4])
    drain(text_kv.at[pl.ds(0, nx - 1)], send.at[6])
    drain(wts.at[0, 0], send.at[7])
    drain(rows_out.at[pl.ds(0, (plane - 1) * pair_rows), :], send.at[9])
    drain(attn.at[pl.ds(0, nx - 1), 0], send.at[10])
    drain(out_send, send.at[11])

    @pl.when(to_self == 0)
    def _():
        drain(text_send, recv.at[8])
        drain(text_send, send.at[8])

    @pl.when(to_self != 0)
    def _():
        drain(text_send.at[0], recv.at[8])
        drain(text_send.at[0], local.at[0])
        drain(text_send.at[0], send.at[8])

    drain(out_send, recv.at[11])


def per_device(hidden, image_qkv, text_slots, norm_gains, out_weight, gate, owner, plan):
    nx, ny, nz = DIMS
    plane = ny * nz
    blocks = nx * CORES
    tokens, model = hidden.shape[2:]
    inner = image_qkv.shape[-1]
    text_len = text_slots.shape[4]
    group = text_len // nx
    rows_a = group // 2
    rows_b = group - rows_a
    wide = inner // ny
    width = model // blocks
    weight_rows = out_weight.shape[1]
    image_rows = plane * CORES * tokens
    table = jnp.asarray(rope_table(tokens * blocks * plane))
    bf16, f32 = jnp.bfloat16, jnp.float32
    anywhere = pl.BlockSpec(memory_space=pl.ANY)
    dma = pltpu.SemaphoreType.DMA
    return pl.pallas_call(
        functools.partial(kernel, DIMS),
        out_shape=(
            jax.ShapeDtypeStruct(hidden.shape, bf16),
            jax.ShapeDtypeStruct((1, 1, CORES, group // CORES, HEAD), bf16),
        ),
        in_specs=[anywhere] * 9,
        out_specs=(anywhere, anywhere),
        scratch_shapes=[
            pltpu.SMEM(owner.shape, jnp.int32),
            pltpu.SMEM(plan.shape, jnp.int32),
            pltpu.VMEM(norm_gains.shape[1:], f32),
            pltpu.VMEM(table.shape, f32),
            pltpu.VMEM(gate.shape[1:], f32),
            pltpu.VMEM((CORES, 3, tokens, inner), bf16),
            pltpu.VMEM((CORES, 3, text_len, inner), bf16),
            pltpu.VMEM((3, nx - 1, rows_a, inner), bf16),
            *[pltpu.VMEM((nx, rows_a, inner), bf16)] * 3,
            pltpu.VMEM((3, rows_a, wide), bf16),
            *[pltpu.VMEM((ny, rows_a, wide), bf16)] * 3,
            pltpu.VMEM((3, nx, rows_b, wide), bf16),
            *[pltpu.VMEM((ny, nx, rows_b, wide), bf16)] * 3,
            pltpu.VMEM((3, nx - 1, rows_b, wide), bf16),
            *[pltpu.VMEM((nx, rows_b, wide), bf16)] * 3,
            pltpu.VMEM((3, nz, group, HEAD), bf16),
            *[pltpu.VMEM((nz, group, HEAD), bf16)] * 3,
            pltpu.VMEM((group, HEAD), bf16),
            pltpu.VMEM((nx, 2, group, HEAD), bf16),
            pltpu.VMEM((plane, CORES, 3, tokens, HEAD), bf16),
            pltpu.VMEM((plane * CORES, 3, tokens, HEAD), bf16),
            pltpu.VMEM((nx, plane * CORES, 2, tokens, HEAD), bf16),
            pltpu.VMEM((image_rows, HEAD), f32),
            pltpu.VMEM((image_rows, HEAD), f32),
            pltpu.VMEM((image_rows, HEAD), bf16),
            pltpu.VMEM((CORES, group // CORES, HEAD), bf16),
            pltpu.VMEM((nx, CORES, CORES * tokens, inner), bf16),
            pltpu.VMEM((nz, ny, blocks, weight_rows, width), bf16),
            pltpu.VMEM((blocks, CORES, tokens, width), bf16),
            pltpu.VMEM((blocks * CORES * tokens, width), f32),
            pltpu.VMEM((blocks, CORES, tokens, width), bf16),
            dma((12,)),
            dma((12,)),
            dma((12,)),
            dma((6, 3)),
            dma((6, 3)),
            dma((3,)),
            dma((2, nz // 2)),
            dma((2, nz // 2)),
            dma((2, nx)),
        ],
        compiler_params=pltpu.CompilerParams(
            collective_id=0, has_side_effects=True, vmem_limit_bytes=60 * 2**20
        ),
    )(
        owner,
        plan,
        norm_gains,
        table,
        gate,
        image_qkv.transpose(0, 1, 3, 2, 4),
        hidden,
        text_slots,
        out_weight,
    )


def solution(mesh):
    return jax.shard_map(
        per_device,
        mesh=mesh,
        in_specs=(
            P("section", None, "seq", None),
            P("section", None, "seq", None, None),
            P("section", None, "seq", None, None, None),
            P("section", None, None),
            P("section", "seq", None),
            P("section", None, None),
            P(),
            P(),
        ),
        out_specs=(P("section", None, "seq", None), P("section", "seq", None, None, None)),
        check_vma=False,
    )
```

time: 117 us -> 93.7 us (0.80)
  Pallas kernels: 108 us -> 90 us
  local copies, waits for them, and re-layouts: 7.79 us -> 2.94 us
    pallas_call x1, Pallas kernels: 108 us -> 90 us  [per_device(): pl.pallas_call(functools.partial(kernel, DIMS), out_shape=(jax.ShapeDtype...]
    unnamed x18 -> x2, local copies, waits for them, and re-layouts: 7.79 us -> 2.94 us
where the time goes in v2:
time: 93.7 us; the launch traced here: 93.6 us
  Pallas kernels  90 us (96%)
  local copies, waits for them, and re-layouts  2.94 us (3%)
    pallas_call x1, Pallas kernels, per_device(): pl.pallas_call(functools.partial(kernel, DIMS), out_shape=(jax.ShapeDtype...  90 us
    unnamed x2, local copies, waits for them, and re-layouts  2.94 us

profile of v2, /device:TPU:1, one launch (start us, length us, event | category | flops | bytes accessed | tf_op | source)
XLA Modules:
  0.0 93.6 jit_solution(17423136067684348157)
XLA Ops:
  0.6 90.0 %shard_map.104 = (bf16[1,2,16,3072]{3,2,1,0:T(8,128)(2,1)}, bf16[1,1,2,32,128]{4,3,2,1,0:T(8,128)(2,1)}) custom-call(s32[4]{0:T(128)} %owner_hbm.1, s32[4]{0:T(128)} %plan_hbm.1, f32[1,4,128]{2,1,0:T(4,128)} %gains_hbm.1, f32[2,144,128]{2,1,0:T(8,128)} %constant.2.clone.table_hbm, f32[1,4,3072]{2,1,0:T(4,128)} %gate_hbm.1, ...), custom_call_target="tpu_custom_call" | custom-call | tf_op jit(solution)/shard_map/pallas_call | solution.py:594
  90.6 1.6 %copy.13 = bf16[1,2,16,3072]{3,2,1,0:T(8,128)(2,1)} copy(bf16[1,2,16,3072]{3,2,1,0:T(8,128)(2,1)} %get-tuple-element.4) | data formatting | bytes 393216
  92.2 1.3 %copy.14 = bf16[1,1,2,32,128]{4,3,2,1,0:T(8,128)(2,1)} copy(bf16[1,1,2,32,128]{4,3,2,1,0:T(8,128)(2,1)} %get-tuple-element.5) | data formatting | bytes 32768

commit v3 on v2

--- a/solution.py
+++ b/solution.py
@@ -69,19 +69,27 @@
     gate_ref,
     qkv_ref,
     slots,
-    a1_out,
+    a1_out_0,
+    a1_out_1,
+    a1_out_2,
     a1_0,
     a1_1,
     a1_2,
-    a2_out,
+    a2_out_0,
+    a2_out_1,
+    a2_out_2,
     a2_0,
     a2_1,
     a2_2,
-    b1_out,
+    b1_out_0,
+    b1_out_1,
+    b1_out_2,
     b1_0,
     b1_1,
     b1_2,
-    b2_out,
+    b2_out_0,
+    b2_out_1,
+    b2_out_2,
     b2_0,
     b2_1,
     b2_2,
@@ -131,7 +139,10 @@
     half = group // CORES
     a1, a2, b1, b2 = (a1_0, a1_1, a1_2), (a2_0, a2_1, a2_2), (b1_0, b1_1, b1_2), (b2_0, b2_1, b2_2)
     z_in = z_in_0, z_in_1, z_in_2
-    rows_a, rows_b, wide = a1_0.shape[1], b1_0.shape[2], b1_0.shape[3]
+    a1_out, a2_out = (a1_out_0, a1_out_1, a1_out_2), (a2_out_0, a2_out_1, a2_out_2)
+    b1_out, b2_out = (b1_out_0, b1_out_1, b1_out_2), (b2_out_0, b2_out_1, b2_out_2)
+    rows_a, rows_b = [ref.shape[1] for ref in a1], [ref.shape[2] for ref in b1]
+    wide = b1_0.shape[3]
     width = hid.shape[-1]
     inner = attn.shape[-1]
     scale = math.log2(math.e) / math.sqrt(HEAD)
@@ -228,29 +239,29 @@
         for dx in sorted(range(nx), key=lambda d: -min(d, nx - d)):
             x_ = (x + dx) % nx
             if dx == 0:
-                fill(a1[t].at[x], x_ * group, rows_a, 0, inner)
+                fill(a1[t].at[x], x_ * group, rows_a[t], 0, inner)
             else:
-                fill(a1_out.at[t, dx - 1], x_ * group, rows_a, 0, inner)
+                fill(a1_out[t].at[dx - 1], x_ * group, rows_a[t], 0, inner)
                 remote(
-                    a1_out.at[t, dx - 1], a1[t].at[x], t_send.at[1, t], t_recv.at[1, t],
+                    a1_out[t].at[dx - 1], a1[t].at[x], t_send.at[1, t], t_recv.at[1, t],
                     at(x_, yz, core),
                 )
 
         @pl.loop(0, nx)
         def _(g):
-            fill(b1_out.at[t, g], g * group + rows_a, rows_b, far * wide, wide)
-            fill(b1[t].at[y, g], g * group + rows_a, rows_b, y * wide, wide)
+            fill(b1_out[t].at[g], g * group + rows_a[t], rows_b[t], far * wide, wide)
+            fill(b1[t].at[y, g], g * group + rows_a[t], rows_b[t], y * wide, wide)
 
         remote(
-            b1_out.at[t], b1[t].at[y], t_send.at[2, t], t_recv.at[2, t],
+            b1_out[t], b1[t].at[y], t_send.at[2, t], t_recv.at[2, t],
             at(x, far * nz + z, core),
         )
 
     def cross(t):
         drain(a1[t].at[pl.ds(0, nx - 1)], t_recv.at[1, t])
-        a2_out[t] = a1[t][own_x, :, lanes(far, wide)]
+        a2_out[t][...] = a1[t][own_x, :, lanes(far, wide)]
         remote(
-            a2_out.at[t], a2[t].at[y], t_send.at[3, t], t_recv.at[3, t],
+            a2_out[t], a2[t].at[y], t_send.at[3, t], t_recv.at[3, t],
             at(x, far * nz + z, core),
         )
         a2[t][y] = a1[t][own_x, :, lanes(y, wide)]
@@ -260,9 +271,9 @@
             if dx == 0:
                 b2[t][x] = b1[t][own_y, x_]
             else:
-                b2_out[t, dx - 1] = b1[t][own_y, x_]
+                b2_out[t][dx - 1] = b1[t][own_y, x_]
                 remote(
-                    b2_out.at[t, dx - 1], b2[t].at[x], t_send.at[4, t], t_recv.at[4, t],
+                    b2_out[t].at[dx - 1], b2[t].at[x], t_send.at[4, t], t_recv.at[4, t],
                     at(x_, yz, core),
                 )
 
@@ -271,8 +282,8 @@
         drain(b2[t].at[pl.ds(0, nx - 1)], t_recv.at[4, t])
 
         def fill(dst, z_):
-            dst[pl.ds(0, rows_a), :] = a2[t][own_y, :, lanes(z_, HEAD)]
-            dst[pl.ds(rows_a, rows_b), :] = b2[t][own_x, :, lanes(z_, HEAD)]
+            dst[pl.ds(0, rows_a[t]), :] = a2[t][own_y, :, lanes(z_, HEAD)]
+            dst[pl.ds(rows_a[t], rows_b[t]), :] = b2[t][own_x, :, lanes(z_, HEAD)]
 
         fill(z_in[t].at[z], z)
 
@@ -384,18 +395,15 @@
     spread(order[2])
     ring(0)
     cross(order[0])
+    keys_start()
     ring(1)
     cross(order[1])
     ring(2)
     deal(order[0])
     cross(order[2])
-    ring(3)
-    keys_start()
     deal(order[1])
     deal(order[2])
-    hidden_start()
-    for step in range(4, steps[0] + 1):
-        ring(step)
+    ring(3)
 
     def meet(queries, keys, values):
         scores = lax.dot_general(
@@ -469,6 +477,7 @@
                 )
 
     attn[x, core, :, own_lanes] = rows_out[lanes(yz, pair_rows), :]
+    hidden_start()
 
     text_pair = [text_kv[:, t].reshape(nx * group, HEAD) for t in range(2)]
     text_parts.append(meet(queries, *text_pair))
@@ -492,7 +501,7 @@
             ).start()
 
     drain(rows_out.at[pl.ds(0, (plane - 1) * pair_rows), :], recv.at[9])
-    for dx in range(1, nx):
+    for dx in sorted(range(1, nx), key=lambda d: -min(d, nx - d)):
         remote(
             attn.at[x, core], attn.at[x, core], send.at[10], line_recv.at[0, dx],
             at((x + dx) % nx, yz, core),
@@ -509,6 +518,8 @@
         )
     for dx in range(nx):
         drain(attn.at[0, 0], line_recv.at[1, dx])
+
+    ring(steps[0])
 
     depth = inner // (nx * ny)
     total[...] = jnp.zeros_like(total)
@@ -581,8 +592,7 @@
     inner = image_qkv.shape[-1]
     text_len = text_slots.shape[4]
     group = text_len // nx
-    rows_a = group // 2
-    rows_b = group - rows_a
+    split = [(rows, group - rows) for rows in (group * 3 // 4, group // 2, group // 2)]
     wide = inner // ny
     width = model // blocks
     weight_rows = out_weight.shape[1]
@@ -607,14 +617,14 @@
             pltpu.VMEM(gate.shape[1:], f32),
             pltpu.VMEM((CORES, 3, tokens, inner), bf16),
             pltpu.VMEM((CORES, 3, text_len, inner), bf16),
-            pltpu.VMEM((3, nx - 1, rows_a, inner), bf16),
-            *[pltpu.VMEM((nx, rows_a, inner), bf16)] * 3,
-            pltpu.VMEM((3, rows_a, wide), bf16),
-            *[pltpu.VMEM((ny, rows_a, wide), bf16)] * 3,
-            pltpu.VMEM((3, nx, rows_b, wide), bf16),
-            *[pltpu.VMEM((ny, nx, rows_b, wide), bf16)] * 3,
-            pltpu.VMEM((3, nx - 1, rows_b, wide), bf16),
-            *[pltpu.VMEM((nx, rows_b, wide), bf16)] * 3,
+            *[pltpu.VMEM((nx - 1, a, inner), bf16) for a, _ in split],
+            *[pltpu.VMEM((nx, a, inner), bf16) for a, _ in split],
+            *[pltpu.VMEM((a, wide), bf16) for a, _ in split],
+            *[pltpu.VMEM((ny, a, wide), bf16) for a, _ in split],
+            *[pltpu.VMEM((nx, b, wide), bf16) for _, b in split],
+            *[pltpu.VMEM((ny, nx, b, wide), bf16) for _, b in split],
+            *[pltpu.VMEM((nx - 1, b, wide), bf16) for _, b in split],
+            *[pltpu.VMEM((nx, b, wide), bf16) for _, b in split],
             pltpu.VMEM((3, nz, group, HEAD), bf16),
             *[pltpu.VMEM((nz, group, HEAD), bf16)] * 3,
             pltpu.VMEM((group, HEAD), bf16),

time: 93.7 us -> 90.1 us (0.962)
  Pallas kernels: 90 us -> 86.3 us
    pallas_call x1, Pallas kernels: 90 us -> 86.3 us  [per_device(): pl.pallas_call(functools.partial(kernel, DIMS), out_shape=(jax.ShapeDtype...]
where the time goes in v3:
time: 90.1 us; the launch traced here: 89.9 us
  Pallas kernels  86.3 us (96%)
  local copies, waits for them, and re-layouts  2.94 us (3%)
    pallas_call x1, Pallas kernels, per_device(): pl.pallas_call(functools.partial(kernel, DIMS), out_shape=(jax.ShapeDtype...  86.3 us
    unnamed x2, local copies, waits for them, and re-layouts  2.94 us

profile of v3, /device:TPU:1, one launch (start us, length us, event | category | flops | bytes accessed | tf_op | source)
XLA Modules:
  0.0 89.9 jit_solution(16664225404986600963)
XLA Ops:
  0.6 86.3 %shard_map.104 = (bf16[1,2,16,3072]{3,2,1,0:T(8,128)(2,1)}, bf16[1,1,2,32,128]{4,3,2,1,0:T(8,128)(2,1)}) custom-call(s32[4]{0:T(128)} %owner_hbm.1, s32[4]{0:T(128)} %plan_hbm.1, f32[1,4,128]{2,1,0:T(4,128)} %gains_hbm.1, f32[2,144,128]{2,1,0:T(8,128)} %constant.2.clone.table_hbm, f32[1,4,3072]{2,1,0:T(4,128)} %gate_hbm.1, ...), custom_call_target="tpu_custom_call" | custom-call | tf_op jit(solution)/shard_map/pallas_call | solution.py:604
  86.9 1.6 %copy.13 = bf16[1,2,16,3072]{3,2,1,0:T(8,128)(2,1)} copy(bf16[1,2,16,3072]{3,2,1,0:T(8,128)(2,1)} %get-tuple-element.4) | data formatting | bytes 393216
  88.6 1.3 %copy.14 = bf16[1,1,2,32,128]{4,3,2,1,0:T(8,128)(2,1)} copy(bf16[1,1,2,32,128]{4,3,2,1,0:T(8,128)(2,1)} %get-tuple-element.5) | data formatting | bytes 32768

commit v4 on v3

--- a/solution.py
+++ b/solution.py
@@ -166,7 +166,6 @@
         (gains_hbm.at[0], gains_ref),
         (owner_hbm, owner_ref),
         (plan_hbm, plan_ref),
-        (gate_hbm.at[0], gate_ref),
     ]
     loads = [
         pltpu.make_async_copy(src, dst, local.at[3 + i]) for i, (src, dst) in enumerate(loads)
@@ -190,6 +189,11 @@
     for x_ in range(nx):
         for c in range(CORES):
             greet(at(x_, yz, c), 1 - section)
+
+    @pl.loop(1, plane)
+    def _(i):
+        greet(at(x, lax.rem(yz + i, plane), core), 1 - section)
+
     per_head = nx * CORES
     for m in range(CORES):
         source = at((seq % per_head) // CORES, seq // per_head, m)
@@ -208,7 +212,7 @@
     own_y, own_z = own_yz // nz, own_yz % nz
 
     pl.semaphore_wait(
-        barrier, plane * CORES - 1 + CORES * (nx - 1) + CORES * nx + CORES - to_self
+        barrier, plane * CORES - 1 + CORES * (nx - 1) + CORES * nx + plane - 1 + CORES - to_self
     )
 
     order = (1, 2, 0)
@@ -301,26 +305,27 @@
             for dc in range(CORES):
                 x_, c_ = (x + dx) % nx, (core + dc) % CORES
                 columns = lanes(x_ * CORES + c_, width)
-                weight_from, weight_to = weight_ref.at[0, :, columns], wts.at[z, y, block]
-                if dx == 0 and dc == 0:
-                    pltpu.make_async_copy(weight_from, weight_to, local.at[0]).start()
-                else:
-                    remote(weight_from, weight_to, send.at[0], recv.at[0], at(x_, yz, c_))
+                remote(
+                    weight_ref.at[0, :, columns], wts.at[z, y, block], send.at[0], recv.at[0],
+                    at(x_, yz, c_), 1 - section,
+                )
+        remote(
+            gate_hbm.at[0, :, lanes(block, width)], gate_ref, send.at[5], recv.at[5], seq,
+            1 - section,
+        )
 
     def hidden_start():
         for dx in range(nx):
             for dc in range(CORES):
                 x_, c_ = (x + dx) % nx, (core + dc) % CORES
                 columns = lanes(x_ * CORES + c_, width)
-                hidden_from, hidden_to = hidden_ref.at[0, :, :, columns], hid.at[block]
-                if dx == 0 and dc == 0:
-                    pltpu.make_async_copy(hidden_from, hidden_to, local.at[1]).start()
-                else:
-                    remote(hidden_from, hidden_to, send.at[1], recv.at[1], at(x_, yz, c_))
+                remote(
+                    hidden_ref.at[0, :, :, columns], hid.at[block], send.at[1], recv.at[1],
+                    at(x_, yz, c_), 1 - section,
+                )
 
     def weights_over_y():
-        drain(wts.at[0, 0, 0], local.at[0])
-        drain(wts.at[0, 0, pl.ds(0, blocks - 1)], recv.at[0])
+        drain(wts.at[0, 0], recv.at[0])
         remote(wts.at[z, y], wts.at[z, y], send.at[7], recv.at[7], at(x, far * nz + z, core))
 
     steps = (nz // 2, (nz - 1) // 2)
@@ -469,14 +474,11 @@
         for k in range(row_block // pair_rows):
             there = index * (row_block // pair_rows) + k
 
-            @pl.when(there != yz)
-            def _():
-                remote(
-                    rows_out.at[lanes(there, pair_rows), :], attn.at[x, core, :, own_lanes],
-                    send.at[9], recv.at[9], at(x, there, core),
-                )
-
-    attn[x, core, :, own_lanes] = rows_out[lanes(yz, pair_rows), :]
+            remote(
+                rows_out.at[lanes(there, pair_rows), :], attn.at[x, core, :, own_lanes],
+                send.at[9], recv.at[9], at(x, there, core), 1 - section,
+            )
+
     hidden_start()
 
     text_pair = [text_kv[:, t].reshape(nx * group, HEAD) for t in range(2)]
@@ -500,7 +502,7 @@
                 text_send.at[part], text_out_ref.at[0, 0, core], local.at[0]
             ).start()
 
-    drain(rows_out.at[pl.ds(0, (plane - 1) * pair_rows), :], recv.at[9])
+    drain(rows_out, recv.at[9])
     for dx in sorted(range(1, nx), key=lambda d: -min(d, nx - d)):
         remote(
             attn.at[x, core], attn.at[x, core], send.at[10], line_recv.at[0, dx],
@@ -530,23 +532,32 @@
         right = wts[:, k % ny, pl.ds((k // ny) * CORES, CORES)].reshape(depth, width)
         total[...] += jnp.dot(left, right, preferred_element_type=jnp.float32)
 
-    drain(hid.at[0], local.at[1])
-    drain(hid.at[pl.ds(0, blocks - 1)], recv.at[1])
+    drain(hid, recv.at[1])
+    drain(gate_ref, recv.at[5])
     columns = lanes(block, width)
 
     @pl.loop(0, blocks)
     def _(dest):
         x_, c_ = dest // CORES, dest % CORES
         for m in range(CORES):
-            gate_row = gate_ref[pl.ds(plan_ref[section * CORES + m], 1), columns]
+            gate_row = gate_ref[pl.ds(plan_ref[(1 - section) * CORES + m], 1), :]
             rows = lanes((x_ * CORES + m) * CORES + c_, tokens)
             out_send[dest, m] = (
                 hid[dest, m].astype(jnp.float32) + gate_row * total[rows, :]
             ).astype(jnp.bfloat16)
-        remote(
-            out_send.at[dest], handed_ref.at[0, :, :, columns], send.at[11], recv.at[11],
-            at(x_, yz, c_), 1 - section,
-        )
+
+        @pl.when(dest != block)
+        def _():
+            remote(
+                out_send.at[dest], handed_ref.at[0, :, :, columns], send.at[11], recv.at[11],
+                at(x_, yz, c_),
+            )
+
+        @pl.when(dest == block)
+        def _():
+            pltpu.make_async_copy(
+                out_send.at[dest], handed_ref.at[0, :, :, columns], local.at[1]
+            ).start()
 
     for t in range(3):
         drain(slots.at[0, t], t_send.at[0, t])
@@ -559,16 +570,18 @@
         for way in range(2):
             if step < steps[way]:
                 drain(wts.at[0], ring_send.at[way, step])
-    drain(wts.at[0, 0, pl.ds(0, blocks - 1)], send.at[0])
-    drain(hid.at[pl.ds(0, blocks - 1)], send.at[1])
+    drain(wts.at[0, 0], send.at[0])
+    drain(hid, send.at[1])
+    drain(gate_ref, send.at[5])
     drain(qkv_recv.at[pl.ds(0, plane * CORES - 1)], send.at[2])
     drain(attn.at[:, 0], send.at[3])
     drain(image_kv.at[pl.ds(0, nx - 1)], send.at[4])
     drain(text_kv.at[pl.ds(0, nx - 1)], send.at[6])
     drain(wts.at[0, 0], send.at[7])
-    drain(rows_out.at[pl.ds(0, (plane - 1) * pair_rows), :], send.at[9])
+    drain(rows_out, send.at[9])
     drain(attn.at[pl.ds(0, nx - 1), 0], send.at[10])
-    drain(out_send, send.at[11])
+    drain(out_send.at[pl.ds(0, blocks - 1)], send.at[11])
+    drain(out_send.at[0], local.at[1])
 
     @pl.when(to_self == 0)
     def _():
@@ -581,7 +594,7 @@
         drain(text_send.at[0], local.at[0])
         drain(text_send.at[0], send.at[8])
 
-    drain(out_send, recv.at[11])
+    drain(out_send.at[pl.ds(0, blocks - 1)], recv.at[11])
 
 
 def per_device(hidden, image_qkv, text_slots, norm_gains, out_weight, gate, owner, plan):
@@ -614,7 +627,7 @@
             pltpu.SMEM(plan.shape, jnp.int32),
             pltpu.VMEM(norm_gains.shape[1:], f32),
             pltpu.VMEM(table.shape, f32),
-            pltpu.VMEM(gate.shape[1:], f32),
+            pltpu.VMEM((gate.shape[1], width), f32),
             pltpu.VMEM((CORES, 3, tokens, inner), bf16),
             pltpu.VMEM((CORES, 3, text_len, inner), bf16),
             *[pltpu.VMEM((nx - 1, a, inner), bf16) for a, _ in split],

time: 90.1 us -> 89.2 us (0.990)
  no operation moved by 1% of the time
where the time goes in v4:
time: 89.2 us; the launch traced here: 89 us
  Pallas kernels  85.5 us (96%)
  local copies, waits for them, and re-layouts  2.94 us (3%)
    pallas_call x1, Pallas kernels, per_device(): pl.pallas_call(functools.partial(kernel, DIMS), out_shape=(jax.ShapeDtype...  85.5 us
    unnamed x2, local copies, waits for them, and re-layouts  2.94 us

profile of v4, /device:TPU:1, one launch (start us, length us, event | category | flops | bytes accessed | tf_op | source)
XLA Modules:
  0.0 89.0 jit_solution(9128195839732056115)
XLA Ops:
  0.6 85.5 %shard_map.104 = (bf16[1,2,16,3072]{3,2,1,0:T(8,128)(2,1)}, bf16[1,1,2,32,128]{4,3,2,1,0:T(8,128)(2,1)}) custom-call(s32[4]{0:T(128)} %owner_hbm.1, s32[4]{0:T(128)} %plan_hbm.1, f32[1,4,128]{2,1,0:T(4,128)} %gains_hbm.1, f32[2,144,128]{2,1,0:T(8,128)} %constant.2.clone.table_hbm, f32[1,4,3072]{2,1,0:T(4,128)} %gate_hbm.1, ...), custom_call_target="tpu_custom_call" | custom-call | tf_op jit(solution)/shard_map/pallas_call | solution.py:617
  86.1 1.6 %copy.13 = bf16[1,2,16,3072]{3,2,1,0:T(8,128)(2,1)} copy(bf16[1,2,16,3072]{3,2,1,0:T(8,128)(2,1)} %get-tuple-element.4) | data formatting | bytes 393216
  87.7 1.3 %copy.14 = bf16[1,1,2,32,128]{4,3,2,1,0:T(8,128)(2,1)} copy(bf16[1,1,2,32,128]{4,3,2,1,0:T(8,128)(2,1)} %get-tuple-element.5) | data formatting | bytes 32768

commit v5 on v4

--- a/solution.py
+++ b/solution.py
@@ -364,14 +364,20 @@
     def keys_start():
         drain(qkv_recv.at[pl.ds(0, plane * CORES - 1)], recv.at[2])
         drain(qkv_recv.at[0], local.at[2])
-        for dx in range(1, nx):
+        for dx, sem in ((1, recv.at[4]), (nx - 1, recv.at[3])):
             remote(
-                qkv_recv.at[:, pl.ds(1, 2)], image_kv.at[x], send.at[4], recv.at[4],
+                qkv_recv.at[:, pl.ds(1, 2)], image_kv.at[x], send.at[4], sem,
                 at((x + dx) % nx, yz, core),
             )
         pltpu.make_async_copy(
             qkv_recv.at[:, pl.ds(1, 2)], image_kv.at[x], local.at[2]
         ).start()
+
+    def keys_forward():
+        for dx, sem, part in ((1, recv.at[4], 0), (nx - 1, recv.at[3], 1)):
+            drain(image_kv.at[0], sem)
+            piece = image_kv.at[(x + nx - dx) % nx, pl.ds(part * plane, plane)]
+            remote(piece, piece, send.at[4], recv.at[10], at((x + dx) % nx, yz, core))
 
     weights_start()
     spread(order[0])
@@ -406,6 +412,7 @@
     ring(2)
     deal(order[0])
     cross(order[2])
+    keys_forward()
     deal(order[1])
     deal(order[2])
     ring(3)
@@ -433,7 +440,7 @@
     def image_pair(x_):
         return [image_kv[x_, :, t].reshape(image_rows, HEAD) for t in range(2)]
 
-    drain(image_kv.at[pl.ds(0, nx - 1)], recv.at[4])
+    drain(image_kv.at[0], recv.at[10])
     drain(image_kv.at[0], local.at[2])
 
     @pl.loop(0, image_rows // row_block)

time: 89.2 us -> 84.3 us (0.945)
  Pallas kernels: 85.5 us -> 80.5 us
    pallas_call x1, Pallas kernels: 85.5 us -> 80.5 us  [per_device(): pl.pallas_call(functools.partial(kernel, DIMS), out_shape=(jax.ShapeDtype...]
where the time goes in v5:
time: 84.3 us; the launch traced here: 84.1 us
  Pallas kernels  80.5 us (95%)
  local copies, waits for them, and re-layouts  2.94 us (3%)
    pallas_call x1, Pallas kernels, per_device(): pl.pallas_call(functools.partial(kernel, DIMS), out_shape=(jax.ShapeDtype...  80.5 us
    unnamed x2, local copies, waits for them, and re-layouts  2.94 us

profile of v5, /device:TPU:1, one launch (start us, length us, event | category | flops | bytes accessed | tf_op | source)
XLA Modules:
  0.0 84.1 jit_solution(2046745794461747761)
XLA Ops:
  0.6 80.5 %shard_map.104 = (bf16[1,2,16,3072]{3,2,1,0:T(8,128)(2,1)}, bf16[1,1,2,32,128]{4,3,2,1,0:T(8,128)(2,1)}) custom-call(s32[4]{0:T(128)} %owner_hbm.1, s32[4]{0:T(128)} %plan_hbm.1, f32[1,4,128]{2,1,0:T(4,128)} %gains_hbm.1, f32[2,144,128]{2,1,0:T(8,128)} %constant.2.clone.table_hbm, f32[1,4,3072]{2,1,0:T(4,128)} %gate_hbm.1, ...), custom_call_target="tpu_custom_call" | custom-call | tf_op jit(solution)/shard_map/pallas_call | solution.py:624
  81.2 1.6 %copy.13 = bf16[1,2,16,3072]{3,2,1,0:T(8,128)(2,1)} copy(bf16[1,2,16,3072]{3,2,1,0:T(8,128)(2,1)} %get-tuple-element.4) | data formatting | bytes 393216
  82.8 1.3 %copy.14 = bf16[1,1,2,32,128]{4,3,2,1,0:T(8,128)(2,1)} copy(bf16[1,1,2,32,128]{4,3,2,1,0:T(8,128)(2,1)} %get-tuple-element.5) | data formatting | bytes 32768

commit v6 on v5

--- a/solution.py
+++ b/solution.py
@@ -440,6 +440,17 @@
     def image_pair(x_):
         return [image_kv[x_, :, t].reshape(image_rows, HEAD) for t in range(2)]
 
+    def text_rows_of(t):
+        drain(z_in[t].at[pl.ds(0, nz - 1)], t_recv.at[5, t])
+        return z_in[t][own_z]
+
+    text_kv[x, 0] = normalize(text_rows_of(1), gains_ref[3, :][None, :]).astype(jnp.bfloat16)
+    text_kv[x, 1] = text_rows_of(2)
+    for dx in range(1, nx):
+        remote(
+            text_kv.at[x], text_kv.at[x], send.at[6], recv.at[6], at((x + dx) % nx, yz, core)
+        )
+
     drain(image_kv.at[0], recv.at[10])
     drain(image_kv.at[0], local.at[2])
 
@@ -451,16 +462,6 @@
         num[rows, :] = sum(p[0] for p in parts[1:]) + parts[0][0]
         den[rows, :] = sum(p[1] for p in parts[1:]) + parts[0][1]
 
-    def text_rows_of(t):
-        drain(z_in[t].at[pl.ds(0, nz - 1)], t_recv.at[5, t])
-        return z_in[t][own_z]
-
-    text_kv[x, 0] = normalize(text_rows_of(1), gains_ref[3, :][None, :]).astype(jnp.bfloat16)
-    text_kv[x, 1] = text_rows_of(2)
-    for dx in range(1, nx):
-        remote(
-            text_kv.at[x], text_kv.at[x], send.at[6], recv.at[6], at((x + dx) % nx, yz, core)
-        )
     text_q[...] = normalize(text_rows_of(0), gains_ref[2, :][None, :]).astype(jnp.bfloat16)
     queries = text_q[...]
     text_parts = [meet(queries, *image_pair(x_)) for x_ in range(nx)]

time: 84.3 us -> 84.1 us (level)
  no operation moved by 1% of the time
where the time goes in v6:
time: 84.1 us; the launch traced here: 83.9 us
  Pallas kernels  80.3 us (95%)
  local copies, waits for them, and re-layouts  2.94 us (3%)
    pallas_call x1, Pallas kernels, per_device(): pl.pallas_call(functools.partial(kernel, DIMS), out_shape=(jax.ShapeDtype...  80.3 us
    unnamed x2, local copies, waits for them, and re-layouts  2.94 us

profile of v6, /device:TPU:1, one launch (start us, length us, event | category | flops | bytes accessed | tf_op | source)
XLA Modules:
  0.0 83.9 jit_solution(4165851491460353454)
XLA Ops:
  0.6 80.3 %shard_map.104 = (bf16[1,2,16,3072]{3,2,1,0:T(8,128)(2,1)}, bf16[1,1,2,32,128]{4,3,2,1,0:T(8,128)(2,1)}) custom-call(s32[4]{0:T(128)} %owner_hbm.1, s32[4]{0:T(128)} %plan_hbm.1, f32[1,4,128]{2,1,0:T(4,128)} %gains_hbm.1, f32[2,144,128]{2,1,0:T(8,128)} %constant.2.clone.table_hbm, f32[1,4,3072]{2,1,0:T(4,128)} %gate_hbm.1, ...), custom_call_target="tpu_custom_call" | custom-call | tf_op jit(solution)/shard_map/pallas_call | solution.py:625
  80.9 1.6 %copy.13 = bf16[1,2,16,3072]{3,2,1,0:T(8,128)(2,1)} copy(bf16[1,2,16,3072]{3,2,1,0:T(8,128)(2,1)} %get-tuple-element.4) | data formatting | bytes 393216
  82.5 1.3 %copy.14 = bf16[1,1,2,32,128]{4,3,2,1,0:T(8,128)(2,1)} copy(bf16[1,1,2,32,128]{4,3,2,1,0:T(8,128)(2,1)} %get-tuple-element.5) | data formatting | bytes 32768
